TPU v7x, 512 devices: a whole 4x8x8 slice. The times are simulated.
512 devices in a mesh: seq: 128 (over z_lo, y, x, core), head: 4 (over z_hi).
Axes of the slice: x: 4, y: 8, z: 8 (z_hi: 4, z_lo: 2; z = z_hi * 2 + z_lo), core: 2. Of those that a mesh axis runs over, the one named last changes fastest.
Arguments:
- queries: bfloat16 [16384, 1536], P('seq', 'head'), may hold values from -240 to 240
- key_states: bfloat16 [16384, 1536], P('seq', 'head'), may hold values from -8 to 8
- value_states: bfloat16 [16384, 1536], P('seq', 'head'), may hold values from -6 to 6
- attn_output: bfloat16 [16384, 1536], P('seq', 'head'), may hold values from -6 to 6
- grad_output: bfloat16 [16384, 1536], P('seq', 'head'), may hold values from -6 to 6
- block_index: int32 [128, 4], P('seq'), may hold values from 0 to 31, as said below
- valid_count: int32 [128], P('seq'), may hold values from 1 to 4, 256 in all
Outputs:
- grad_queries: bfloat16 [16384, 1536], P(('seq', 'head'))
- grad_keys: bfloat16 [16384, 1536], P(('seq', 'head'))
- grad_values: bfloat16 [16384, 1536], P(('seq', 'head'))
Inputs may be any that keep to these rules, and one draw needn't show every extreme that they name: `block_index`: each owner's 4 entries are distinct block numbers of its own 128 tokens in blocks of 4; entries at slots from valid_count on are padding. `valid_count`: the counts sum to 256.
All inputs are finite; a program needn't handle non-finite values. No bound on the sum of `valid_count` on one device may be relied on, other than what follows from the above.
Results may differ from a plain program's by a relative error of at most 0.017.
Values may be sent and summed in bfloat16 or wider, within the bound.
A program may use at most 64 MiB of HBM per device.

v0:
```python
import jax
import jax.numpy as jnp
from jax import lax
from jax.sharding import PartitionSpec as P

HD = 128
BLK = 4
MB_DEV = 4


def key_scores(query_block, key_heads, score_scale):
    query_heads = query_block.reshape(query_block.shape[0], key_heads.shape[1], HD)
    return (
        jnp.einsum("qhd,khd->hqk", query_heads, key_heads, preferred_element_type=jnp.float32)
        * score_scale
    )


def log_totals(query_blocks, key_heads, score_scale):

    def block_stats(query_block):
        scores = key_scores(query_block, key_heads, score_scale)
        peak = jnp.max(scores, axis=2)
        summed = jnp.sum(jnp.exp(scores - peak[:, :, None]), axis=2)
        return (peak, summed)

    peak, summed = lax.map(block_stats, query_blocks)
    highest = lax.pmax(peak, "seq")
    summed = lax.psum(summed * jnp.exp(peak - highest), "seq")
    peak = highest
    return peak + jnp.log(summed)


def attend(all_queries, all_grads, all_delta, key_states, value_states):
    key_rows, feat_width = key_states.shape
    heads_here = feat_width // HD
    score_scale = HD ** (-0.5)
    key_heads = key_states.reshape(key_rows, heads_here, HD)
    value_heads = value_states.reshape(key_rows, heads_here, HD)
    total_rows = all_queries.shape[0]
    block_rows = min(512, total_rows)
    block_count = total_rows // block_rows
    query_blocks = all_queries.reshape(block_count, block_rows, feat_width)
    log_total = log_totals(query_blocks, key_heads, score_scale)

    def advance(carried, pieces):
        grad_k, grad_v = carried
        query_block, grad_block, delta_block, total_block = pieces
        scores = key_scores(query_block, key_heads, score_scale)
        weights = jnp.exp(scores - total_block[:, :, None])
        weights_low = weights.astype(jnp.bfloat16)
        grad_heads = grad_block.reshape(block_rows, heads_here, HD)
        grad_v = grad_v + jnp.einsum(
            "hqk,qhd->khd", weights_low, grad_heads, preferred_element_type=jnp.float32
        )
        dprobs = jnp.einsum(
            "qhd,khd->hqk", grad_heads, value_heads, preferred_element_type=jnp.float32
        )
        dscores = (weights * (dprobs - delta_block.astype(jnp.float32).T[:, :, None])).astype(
            jnp.bfloat16
        )
        query_heads = query_block.reshape(block_rows, heads_here, HD)
        grad_q = (
            jnp.einsum("hqk,khd->qhd", dscores, key_heads, preferred_element_type=jnp.float32)
            * score_scale
        )
        grad_k = (
            grad_k
            + jnp.einsum("hqk,qhd->khd", dscores, query_heads, preferred_element_type=jnp.float32)
            * score_scale
        )
        return ((grad_k, grad_v), grad_q.reshape(block_rows, feat_width))

    empty_acc = jnp.zeros((key_rows, heads_here, HD), jnp.float32)
    pieces = (
        query_blocks,
        all_grads.reshape(block_count, block_rows, feat_width),
        all_delta.reshape(block_count, block_rows, heads_here),
        log_total,
    )
    (grad_k, grad_v), grad_q = lax.scan(advance, (empty_acc, empty_acc), pieces)
    return (
        grad_q.reshape(total_rows, feat_width),
        grad_k.reshape(key_rows, feat_width).astype(jnp.bfloat16),
        grad_v.reshape(key_rows, feat_width).astype(jnp.bfloat16),
    )


def body(queries, key_states, value_states, attn_output, grad_output, block_index, valid_count):
    key_rows, feat_width = key_states.shape
    heads_here = feat_width // HD
    slots = MB_DEV * BLK
    owned_blocks = block_index[0]
    owned_count = valid_count[0]
    offsets = jnp.arange(BLK, dtype=jnp.int32)
    row_ids = (owned_blocks[:, None] * BLK + offsets[None, :]).reshape(slots)
    slot_live = jnp.repeat(jnp.arange(MB_DEV, dtype=jnp.int32) < owned_count, BLK)[:, None]
    nothing = jnp.zeros((), jnp.bfloat16)
    own_queries = jnp.where(slot_live, jnp.take(queries, row_ids, axis=0), nothing)
    own_grads = jnp.where(slot_live, jnp.take(grad_output, row_ids, axis=0), nothing)
    own_output = jnp.take(attn_output, row_ids, axis=0)
    products = own_grads.astype(jnp.float32).reshape(slots, heads_here, HD) * own_output.astype(
        jnp.float32
    ).reshape(slots, heads_here, HD)
    row_delta = jnp.sum(products, axis=2).astype(jnp.bfloat16)
    gathered = (
        lax.all_gather(own_queries, "seq", axis=0, tiled=True),
        lax.all_gather(own_grads, "seq", axis=0, tiled=True),
        lax.all_gather(row_delta, "seq", axis=0, tiled=True),
    )
    grad_terms, grad_k, grad_v = attend(
        gathered[0], gathered[1], gathered[2], key_states, value_states
    )
    own_dq = lax.psum_scatter(grad_terms, "seq", scatter_dimension=0, tiled=True).astype(
        jnp.bfloat16
    )
    placed = (
        jnp.zeros((key_rows, feat_width), jnp.bfloat16)
        .at[row_ids]
        .set(jnp.where(slot_live, own_dq, nothing))
    )
    result = (
        lax.all_to_all(placed, "head", split_axis=0, concat_axis=1, tiled=True),
        lax.all_to_all(grad_k, "head", split_axis=0, concat_axis=1, tiled=True),
        lax.all_to_all(grad_v, "head", split_axis=0, concat_axis=1, tiled=True),
    )
    return (result[0], result[1], result[2])


def solution(mesh):
    in_specs = (
        P("seq", "head"),
        P("seq", "head"),
        P("seq", "head"),
        P("seq", "head"),
        P("seq", "head"),
        P("seq", None),
        P("seq"),
    )
    out_specs = (P(("seq", "head"), None), P(("seq", "head"), None), P(("seq", "head"), None))
    return jax.shard_map(body, mesh=mesh, in_specs=in_specs, out_specs=out_specs, check_vma=False)
```

profile of v0, /device:TPU:1, one launch (start us, length us, event | category | flops | bytes accessed | tf_op | source)
XLA Modules:
  0.0 1946.4 jit_solution(13348321397965189564)
XLA Ops:
  7.2 0.7 multiply_bitcast_fusion
  9.5 0.7 select_select_fusion.1
  10.3 1.5 gather_fusion.2
  11.8 1.5 gather_fusion.1
  13.3 0.7 convert_multiply_fusion
  14.3 1.0 copy.85
  15.4 1.0 copy.88
  16.5 0.8 copy.93
  17.2 159.6 %all-gather = bf16[128,16,3]{1,2,0:T(4,128)(2,1)S(1)} all-gather(bf16[1,16,3]{1,2,0:T(4,128)(2,1)S(1)} %bitcast.123), channel_id=1, replica_groups=mesh['seq'=128,'head'=4] {'seq'}, dimensions={0}, use_global_device_ids=true | all-gather | bytes 12384 | tf_op jit(solution)/shard_map/all_gather | solution.py:109
  177.0 52.6 %all-gather.4.cloned.1.call-done = bf16[2048,384]{1,0:T(8,128)(2,1)} async-done(((bf16[16,384]{1,0:T(8,128)(2,1)}), bf16[2048,384]{1,0:T(8,128)(2,1)}) %all-gather.4.cloned.1.call-update) | async-done | bytes 1572880 | tf_op jit(solution)/shard_map/all_gather | solution.py:107
  229.6 1.7 copy.91
  231.3 1.9 while.27
  233.2 547.3 %pmax.7 = f32[4,3,512]{2,1,0:T(4,128)S(1)} all-reduce(f32[4,3,512]{2,1,0:T(4,128)S(1)} %get-tuple-element.86), channel_id=1, replica_groups=mesh['seq'=128,'head'=4] {'seq'}, use_global_device_ids=true, to_apply=%region_5.7 | all-reduce | flops 6144 | bytes 49152 | tf_op jit(solution)/shard_map/pmax | solution.py:28
  780.6 548.4 %psum.7 = f32[4,3,512]{2,1,0:T(4,128)S(1)} all-reduce(f32[4,3,512]{2,1,0:T(4,128)S(1)} %exponential_multiply_fusion), channel_id=1, replica_groups=mesh['seq'=128,'head'=4] {'seq'}, use_global_device_ids=true, to_apply=%region_6.8 | all-reduce | flops 6144 | bytes 49152 | tf_op jit(solution)/shard_map/psum | solution.py:29
  1329.6 29.5 %while.28 = (s32[]{:T(128)}, f32[128,3,128]{0,2,1:T(8,128)}, f32[128,3,128]{0,2,1:T(8,128)S(1)}, f32[4,512,384]{2,1,0:T(8,128)}, bf16[4,512,384]{1,2,0:T(8,128)(...) while((s32[]{:T(128)}, f32[128,3,128]{0,2,1:T(8,128)}, ...), condition=%wide.region_8.10_spmd.clone, body=%wide.region_7.9_spmd.clone.sunk | while | flops 253281792 | bytes 14091420 | solution.py:81
  1329.6 0.7 dynamic-slice_bitcast_fusion.2
  1330.3 1.0 constant_dynamic-slice_fusion.8
  1332.3 1.3 fusion.60
  1333.6 1.0 fusion.61
  1335.3 1.0 constant_dynamic-update-slice_fusion.2
  1336.3 0.7 dynamic-slice_bitcast_fusion.2
  1337.0 1.0 constant_dynamic-slice_fusion.8
  1339.0 1.3 fusion.60
  1340.3 1.9 fusion.61
  1343.0 1.0 constant_dynamic-update-slice_fusion.2
  1343.9 0.7 dynamic-slice_bitcast_fusion.2
  1344.6 1.0 constant_dynamic-slice_fusion.8
  1346.6 1.3 fusion.60
  1347.9 1.9 fusion.61
  1350.6 1.0 constant_dynamic-update-slice_fusion.2
  1351.5 0.7 dynamic-slice_bitcast_fusion.2
  1352.2 1.0 constant_dynamic-slice_fusion.8
  1354.2 1.3 fusion.60
  1355.5 1.9 fusion.61
  1358.2 0.9 constant_dynamic-update-slice_fusion.2
  1359.2 0.9 convert_element_type.40
  1360.3 0.7 convert_element_type.41
  1361.0 6.2 all-to-all-start.1
  1367.4 0.7 convert_element_type.43
  1368.1 6.1 all-to-all-done.1
  1374.2 3.3 all-to-all-start.2
  1377.6 546.9 %reduce-scatter.2.cloned.1.call-done = f32[16,384]{1,0:T(8,128)} async-done(((f32[2048,384]{1,0:T(8,128)}), f32[16,384]{1,0:T(8,128)}) %reduce-scatter.2.cloned.1.call-update) | async-done | bytes 24592 | tf_op jit(solution)/shard_map/reduce_scatter | solution.py:114
  1924.5 1.5 scatter_custom_fusion
  1926.0 6.1 all-to-all-start
  1932.1 0.7 copy.111
  1932.8 0.7 copy.112
  1933.4 5.8 all-to-all-done
  1939.2 0.7 copy.110
  (94 shorter events, 11.2 us)
Async XLA Ops:
  7.2 1.7 copy-start
  7.2 222.4 %all-gather.4.cloned.1.call-start = ((), (), s32[]{:S(2)}) async-start(), calls=%async_computation.4 | async-start | bytes 1585152 | tf_op jit(solution)/shard_map/all_gather | solution.py:107
  8.0 0.9 copy-start.1
  8.9 5.1 copy-start.3
  10.2 1319.4 %all-gather.6.cloned.1.call-start = ((), (), s32[]{:S(2)}) async-start(), calls=%async_computation.5 | async-start | bytes 1585152 | tf_op jit(solution)/shard_map/all_gather | solution.py:108
  14.0 1910.5 %reduce-scatter.2.cloned.1.call-start = ((), (), s32[]{:S(2)}) async-start(), calls=%async_computation.6 | async-start | bytes 3170304 | tf_op jit(solution)/shard_map/reduce_scatter | solution.py:114
  1359.1 8.0 copy-start.2
  1359.1 565.4 %copy-start.4 = (pred[16]{0:T(512)(128)(4,1)S(1)}, pred[16]{0:T(512)(128)(4,1)}, u32[]{:S(2)}) copy-start(pred[16]{0:T(512)(128)(4,1)} %copy-done.3) | copy-start | bytes 52
  1361.0 13.2 all-to-all-start.1
  1374.2 551.8 %all-to-all-start.2 = ((bf16[4,32,384]{2,1,0:T(8,128)(2,1)}), bf16[4,32,384]{2,1,0:T(8,128)(2,1)S(1)}, u32[]{:S(2)}, u32[]{:S(2)}) async-start(bf16[4,32,384]{2,1,0:T(8,128)(2,1)} %convert_element_type.43), calls=%async_computation.3 | async-start | bytes 196608 | tf_op jit(solution)/shard_map/all_to_all | solution.py:125
  1926.0 13.1 all-to-all-start
Sparse Core Ops, SparseCore 0:
  10.7 218.7 all-gather.3
  232.3 214.6 all-gather.5
  1359.3 565.1 reduce-scatter.1
where the time goes:
time: 1950 us
  blocking collectives  1260 us (65%)
  waiting for transfers between devices  611 us (31%)
  local copies, waits for them, and re-layouts  26.5 us (1%)
    psum x1, blocking collectives, log_totals(): summed = lax.psum(summed * jnp.exp(peak - highest), 'seq')  548 us
    pmax x1, blocking collectives, log_totals(): highest = lax.pmax(peak, 'seq')  547 us
    reduce_scatter x1, waiting for transfers between devices, body(): lax.psum_scatter(grad_terms, 'seq', scatter_dimension=0, tiled=True)  547 us
    all_gather x1, blocking collectives, body(): lax.all_gather(row_delta, 'seq', axis=0, tiled=True)  160 us
    all_gather x1, waiting for transfers between devices, body(): lax.all_gather(own_queries, 'seq', axis=0, tiled=True)  52.6 us
  transfers between devices with their start and end apart: 6, of which 4 were waited for; matrix products, arithmetic and copies ran while one was open for 1% of the time, Pallas kernels for 0%

commit v1 on v0

v1 whole, which is shorter than its diff:
```python
import functools

import jax
import jax.numpy as jnp
from jax import lax
from jax.experimental import pallas as pl
from jax.experimental.pallas import tpu as pltpu
from jax.sharding import PartitionSpec as P

HD = 128
BLK = 4
MB_DEV = 4
HL = 3
FEAT = HL * HD
SLOTS = MB_DEV * BLK
TOK = 128
WIDE = 2 * FEAT + HD
KEYS = 4 * TOK
SCALE = HD ** (-0.5)
LOG2E = 1.4426950408889634
MESH = pl.DeviceIdType.MESH
NT = (((1,), (1,)), ((), ()))
NN = (((1,), (0,)), ((), ()))


def mm(a, b, dims):
    return lax.dot_general(a, b, dims, preferred_element_type=jnp.float32)


def cols(hh):
    return slice(hh * HD, (hh + 1) * HD)


def kernel(
    X, Y, H,
    bi_ref, vc_ref, q_ref, k_ref, v_ref, o_ref, g_ref,
    gq_ref, gk_ref, gv_ref,
    gbuf, kbuf, vbuf, kt, ebuf, dbuf, dqt, mrow, frow, srow, srow2, sxb, syb,
    dqs, rxb, dqo, dys, ryb, dqf, gpart, crecv, fsend, frecv,
    ysend, yrecv, xsend, xrecv, kvsend, kvrecv, ssx, srx, ssy, sry,
    dxs, dxr, dss, dsr, css, csr, fss, fsr, hss, hsr,
):
    C = Y * SLOTS
    s = lax.axis_index("seq")
    h = lax.axis_index("head")
    c = lax.rem(s, 2)
    x = lax.rem(s // 2, X)
    y = lax.rem(s // (2 * X), Y)
    z = s // (2 * X * Y)

    def dev(z_, y_, x_, c_, h_):
        return {"seq": ((z_ * Y + y_) * X + x_) * 2 + c_, "head": h_}

    def up(v, d, n):
        return lax.rem(v + d, n)

    def dn(v, d, n):
        return lax.rem(v + n - d, n)

    quad = [(0, 1), (1, 0), (1, 1)]
    final = [(dz, dh) for dz in range(2) for dh in range(H) if dz or dh]
    xp = [dev(z, y, up(x, e, X), c, h) for e in range(1, X)]
    yp = [dev(z, up(y, d, Y), x, c, h) for d in range(1, Y)]
    qp = [dev(up(z, dz, 2), y, x, up(c, dc, 2), h) for dz, dc in quad]
    fp = [dev(up(z, dz, 2), y, x, c, up(h, dh, H)) for dz, dh in final]
    extra = [p for p, (dz, dh) in zip(fp, final) if dh]

    barrier = pltpu.get_barrier_semaphore()
    greet = xp + yp + qp + extra
    for p in greet:
        pl.semaphore_signal(barrier, inc=1, device_id=p, device_id_type=MESH)

    def rcopy(src, dst, ss, rs, to):
        return pltpu.make_async_remote_copy(
            src_ref=src, dst_ref=dst, send_sem=ss, recv_sem=rs,
            device_id=to, device_id_type=MESH,
        )

    count = vc_ref[0] * BLK
    b = [bi_ref[0, j] * BLK for j in range(MB_DEV)]

    def targets(idx):
        j = idx // BLK
        t = jnp.where(j == 0, b[0], jnp.where(j == 1, b[1], jnp.where(j == 2, b[2], b[3])))
        return jnp.where(idx < count, t + lax.rem(idx, BLK), -1)

    ri = lax.broadcasted_iota(jnp.int32, (SLOTS, TOK), 0)
    li = lax.broadcasted_iota(jnp.int32, (SLOTS, TOK), 1)
    sel = jnp.where(targets(ri) == li, 1.0, 0.0).astype(jnp.bfloat16)
    own_q = mm(sel, q_ref[...], NN).astype(jnp.bfloat16)
    own_g = mm(sel, g_ref[...], NN)
    own_o = mm(sel, o_ref[...], NN)
    prod = own_g * own_o
    dcol = jnp.zeros((SLOTS, HD), jnp.float32)
    for hh in range(HL):
        dcol = jnp.where(li == hh, jnp.sum(prod[:, cols(hh)], axis=1, keepdims=True), dcol)
    gbuf[0, 0] = jnp.concatenate(
        [own_q, own_g.astype(jnp.bfloat16), dcol.astype(jnp.bfloat16)], axis=1
    )
    kbuf[0] = k_ref[...]
    vbuf[0] = v_ref[...]

    pl.semaphore_wait(barrier, len(greet))

    ysent = []
    for d in [Y // 2] + [t for i in range(1, (Y + 1) // 2) for t in (i, Y - i)]:
        cp = rcopy(gbuf.at[0, 0], gbuf.at[0, d], ysend.at[d - 1], yrecv.at[d - 1], yp[d - 1])
        cp.start()
        ysent.append(cp)
    kvsent = []
    for i, (src, buf) in enumerate(((k_ref, kbuf), (v_ref, vbuf))):
        for j in range(3):
            cp = rcopy(src, buf.at[j + 1], kvsend.at[i, j], kvrecv.at[i, j], qp[j])
            cp.start()
            kvsent.append(cp)
    xsent = []
    order = [0] + [t for i in range(1, (Y + 1) // 2) for t in (i, Y - i)] + [Y // 2]
    for d in order:
        if d:
            rcopy(gbuf.at[0, 0], gbuf.at[0, d], ysend.at[d - 1], yrecv.at[d - 1], yp[d - 1]).wait_recv()
        for e in range(1, X):
            cp = rcopy(gbuf.at[0, d], gbuf.at[e, d], xsend.at[d, e - 1], xrecv.at[d, e - 1], xp[e - 1])
            cp.start()
            xsent.append(cp)

    def kv_wait(i, buf):
        for j in range(3):
            rcopy(k_ref, buf.at[j + 1], kvsend.at[i, j], kvrecv.at[i, j], qp[j]).wait_recv()

    kv_wait(0, kbuf)
    for hh in range(HL):
        kt[hh] = kbuf[:, :, cols(hh)].reshape(KEYS, HD).T

    mrow[...] = jnp.zeros_like(mrow)
    srow[...] = jnp.zeros_like(srow)
    arrive = [0] + [e for e in range(1, X) if e != 2] + ([2] if X > 2 else [])
    for e in arrive:
        if e:
            for d in order:
                rcopy(gbuf.at[0, d], gbuf.at[e, d], xsend.at[d, e - 1], xrecv.at[d, e - 1], xp[e - 1]).wait_recv()
        for hh in range(HL):
            kh = kbuf[:, :, cols(hh)].reshape(KEYS, HD)
            qh = gbuf[e, :, :, cols(hh)].reshape(C, HD)
            s2 = mm(kh, qh, NT) * (SCALE * LOG2E)
            m = jnp.max(s2, axis=0, keepdims=True)
            ex = jnp.exp2(s2 - m)
            tot = jnp.sum(ex, axis=0, keepdims=True)
            ebuf[e, hh] = ex
            n = e * HL + hh
            mrow[n : n + 1, :] = m
            srow[n : n + 1, :] = m + jnp.log2(tot)

    def combine(parts):
        top = functools.reduce(jnp.maximum, parts)
        return top + jnp.log2(sum(jnp.exp2(p - top) for p in parts))

    stat_sent = []
    for e in range(1, X):
        cp = rcopy(srow, sxb.at[e - 1], ssx.at[e - 1], srx.at[e - 1], xp[e - 1])
        cp.start()
        stat_sent.append(cp)

    def dprobs(e):
        for hh in range(HL):
            vh = vbuf[:, :, cols(hh)].reshape(KEYS, HD)
            lane = lax.broadcasted_iota(jnp.int32, (KEYS, HD), 1)
            neg = jnp.where(lane == hh, -1.0, 0.0).astype(jnp.bfloat16)
            gh = gbuf[e, :, :, FEAT + hh * HD : FEAT + (hh + 1) * HD].reshape(C, HD)
            dh = gbuf[e, :, :, 2 * FEAT : WIDE].reshape(C, HD)
            dp = mm(jnp.concatenate([vh, neg], 1), jnp.concatenate([gh, dh], 1), NT)
            dd = ebuf[e, hh] * dp
            dbuf[e, hh] = dd
            dqt[e, hh] = mm(kt[hh], dd.astype(jnp.bfloat16), NN)

    kv_wait(1, vbuf)
    dprobs(0)
    if X > 2:
        dprobs(1)
    for e in range(1, X):
        cp = stat_sent[e - 1]
        cp.wait_recv()
    srow2[...] = srow[...]
    for i in range(X):
        parts = [srow[i * HL : (i + 1) * HL, :]]
        for e in range(1, X):
            n = (i - e) % X * HL
            parts.append(sxb[e - 1, n : n + HL, :])
        srow2[i * HL : (i + 1) * HL, :] = combine(parts)
    for d in range(1, Y):
        cp = rcopy(srow2, syb.at[d - 1], ssy.at[d - 1], sry.at[d - 1], yp[d - 1])
        cp.start()
        stat_sent.append(cp)
    for i in range(2 if X > 2 else 1, X):
        dprobs(i)
    for cp in stat_sent[X - 1 :]:
        cp.wait_recv()
    parts = [srow2[...]] + [pltpu.roll(syb[d - 1], d * SLOTS, 1) for d in range(1, Y)]
    frow[...] = jnp.exp2(mrow[...] - combine(parts))

    dq_sent = []
    for e in ([2] if X > 2 else []) + [e for e in range(1, X) if e != 2] + [0]:
        for hh in range(HL):
            n = e * HL + hh
            t = (dqt[e, hh] * (frow[n : n + 1, :] * SCALE)).T
            if e:
                dqs[e - 1, :, cols(hh)] = t.astype(jnp.bfloat16)
            else:
                dqo[:, cols(hh)] = t
        if e:
            cp = rcopy(dqs.at[e - 1], rxb.at[e - 1], dxs.at[e - 1], dxr.at[e - 1], xp[X - e - 1])
            cp.start()
            dq_sent.append(cp)

    core = dev(z, y, x, 1 - c, h)
    last_sent = []

    def grads(hh):
        f = [frow[i * HL + hh : i * HL + hh + 1, :] for i in range(X)]
        w = jnp.concatenate([(ebuf[i, hh] * f[i]).astype(jnp.bfloat16) for i in range(X)], axis=1)
        gvp = mm(w, gbuf[:, :, :, FEAT + hh * HD : FEAT + (hh + 1) * HD].reshape(X * C, HD), NN)
        ds = jnp.concatenate([(dbuf[i, hh] * f[i]).astype(jnp.bfloat16) for i in range(X)], axis=1)
        gkp = mm(ds, gbuf[:, :, :, cols(hh)].reshape(X * C, HD), NN) * SCALE
        for a, val in enumerate((gkp, gvp)):
            for i in range(4):
                gpart[hh, i % 2, a, i // 2] = val[i * TOK : (i + 1) * TOK].astype(jnp.bfloat16)
        cp = rcopy(gpart.at[hh, 1], crecv.at[hh], css.at[hh], csr.at[hh], core)
        cp.start()
        return cp

    def spread(hh, cp):
        cp.wait_recv()
        for a in range(2):
            for i in range(2):
                tot = gpart[hh, 0, a, i].astype(jnp.float32) + crecv[hh, a, i].astype(jnp.float32)
                fsend[hh, i, :, a] = tot.astype(jnp.bfloat16).reshape(H, TOK // H, HD)
        for n, (dz, dh) in enumerate(final):
            out = rcopy(
                fsend.at[hh, dz, up(h, dh, H)], frecv.at[hh, dz, h],
                fss.at[hh, n], fsr.at[hh, n], fp[n],
            )
            out.start()
            last_sent.append(out)
        frecv[hh, 0, h] = fsend[hh, 0, h]

    c0 = grads(0)
    for cp in dq_sent:
        cp.wait_recv()
    tot = dqo[...]
    for e in range(1, X):
        tot = tot + rxb[e - 1].astype(jnp.float32)
    dys[...] = tot.astype(jnp.bfloat16).reshape(Y, SLOTS, FEAT)
    y_sent = []
    for d in range(1, Y):
        cp = rcopy(dys.at[d], ryb.at[d - 1], dss.at[d - 1], dsr.at[d - 1], yp[Y - d - 1])
        cp.start()
        y_sent.append(cp)
    spread(0, c0)
    c1 = grads(1)
    spread(1, c1)
    for cp in y_sent:
        cp.wait_recv()
    tot = dys[0].astype(jnp.float32)
    for d in range(1, Y):
        tot = tot + ryb[d - 1].astype(jnp.float32)
    dqf[h] = tot.astype(jnp.bfloat16)
    head_sent = []
    for dh in range(1, H):
        to = dev(z, y, x, c, up(h, dh, H))
        cp = rcopy(dqf.at[h], dqf.at[h], hss.at[dh - 1], hsr.at[dh - 1], to)
        cp.start()
        head_sent.append(cp)
    c2 = grads(2)
    spread(2, c2)

    for dh in range(1, H):
        slot = dn(h, dh, H)
        rcopy(dqf.at[slot], dqf.at[slot], hss.at[dh - 1], hsr.at[dh - 1], xp[0]).wait_recv()
    out_rows = TOK // H
    pr = lax.broadcasted_iota(jnp.int32, (out_rows, SLOTS), 0) + h * out_rows
    pj = lax.broadcasted_iota(jnp.int32, (out_rows, SLOTS), 1)
    put = jnp.where(targets(pj) == pr, 1.0, 0.0).astype(jnp.bfloat16)
    for i in range(H):
        gq_ref[:, i * FEAT : (i + 1) * FEAT] = mm(put, dqf[i], NN).astype(jnp.bfloat16)
    for hh in range(HL):
        for n, (dz, dh) in enumerate(final):
            rcopy(
                fsend.at[hh, 0, 0], frecv.at[hh, dz, dn(h, dh, H)],
                fss.at[hh, n], fsr.at[hh, n], fp[n],
            ).wait_recv()
        for i in range(H):
            lanes = slice(i * FEAT + hh * HD, i * FEAT + (hh + 1) * HD)
            for a, ref in enumerate((gk_ref, gv_ref)):
                both = frecv[hh, 0, i, a].astype(jnp.float32) + frecv[hh, 1, i, a].astype(jnp.float32)
                ref[:, lanes] = both.astype(jnp.bfloat16)
    for cp in ysent + kvsent + xsent + stat_sent + dq_sent + [c0, c1, c2] + y_sent + head_sent + last_sent:
        cp.wait_send()


def body(X, Y, H, queries, key_states, value_states, attn_output, grad_output, block_index, valid_count):
    C = Y * SLOTS
    bf, f32 = jnp.bfloat16, jnp.float32
    V = pltpu.VMEM
    D = pltpu.SemaphoreType.DMA
    nf = 2 * H - 1
    scratch = [
        V((X, Y, SLOTS, WIDE), bf),
        V((4, TOK, FEAT), bf),
        V((4, TOK, FEAT), bf),
        V((HL, HD, KEYS), bf),
        V((X, HL, KEYS, C), f32),
        V((X, HL, KEYS, C), f32),
        V((X, HL, HD, C), f32),
        V((16, C), f32),
        V((16, C), f32),
        V((16, C), f32),
        V((16, C), f32),
        V((X - 1, 16, C), f32),
        V((Y - 1, 16, C), f32),
        V((X - 1, C, FEAT), bf),
        V((X - 1, C, FEAT), bf),
        V((C, FEAT), f32),
        V((Y, SLOTS, FEAT), bf),
        V((Y - 1, SLOTS, FEAT), bf),
        V((H, SLOTS, FEAT), bf),
        V((HL, 2, 2, 2, TOK, HD), bf),
        V((HL, 2, 2, TOK, HD), bf),
        V((HL, 2, H, 2, TOK // H, HD), bf),
        V((HL, 2, H, 2, TOK // H, HD), bf),
        D((Y - 1,)), D((Y - 1,)),
        D((Y, X - 1)), D((Y, X - 1)),
        D((2, 3)), D((2, 3)),
        D((X - 1,)), D((X - 1,)),
        D((Y - 1,)), D((Y - 1,)),
        D((X - 1,)), D((X - 1,)),
        D((Y - 1,)), D((Y - 1,)),
        D((HL,)), D((HL,)),
        D((HL, nf)), D((HL, nf)),
        D((H - 1,)), D((H - 1,)),
    ]
    out = jax.ShapeDtypeStruct((TOK // H, H * FEAT), bf)
    vm = pl.BlockSpec(memory_space=pltpu.VMEM)
    sm = pl.BlockSpec(memory_space=pltpu.SMEM)
    return pl.pallas_call(
        functools.partial(kernel, X, Y, H),
        out_shape=(out, out, out),
        in_specs=[sm, sm, vm, vm, vm, vm, vm],
        out_specs=(vm, vm, vm),
        scratch_shapes=scratch,
        compiler_params=pltpu.CompilerParams(
            collective_id=0, has_side_effects=True, vmem_limit_bytes=48 * 1024 * 1024
        ),
    )(block_index, valid_count, queries, key_states, value_states, attn_output, grad_output)


def build(mesh, X, Y):
    H = mesh.shape["head"]
    in_specs = tuple([P("seq", "head")] * 5) + (P("seq", None), P("seq"))
    out_specs = tuple([P(("seq", "head"), None)] * 3)
    return jax.shard_map(
        functools.partial(body, X, Y, H),
        mesh=mesh, in_specs=in_specs, out_specs=out_specs, check_vma=False,
    )


def solution(mesh):
    return build(mesh, 4, 8)
```

time: 1950 us -> 66.2 us (0.03)
  blocking collectives: 1260 us -> 0 us
  waiting for transfers between devices: 611 us -> 0 us
  Pallas kernels: 0 us -> 58.2 us
  local copies, waits for them, and re-layouts: 26.5 us -> 6.38 us
    psum x1 -> x0, blocking collectives: 548 us -> none  [log_totals(): summed = lax.psum(summed * jnp.exp(peak - highest), 'seq')]
    pmax x1 -> x0, blocking collectives: 547 us -> none  [log_totals(): highest = lax.pmax(peak, 'seq')]
    reduce_scatter x1 -> x0, waiting for transfers between devices: 547 us -> none  [body(): lax.psum_scatter(grad_terms, 'seq', scatter_dimension=0, tiled=True)]
    all_gather x1 -> x0, blocking collectives: 160 us -> none  [body(): lax.all_gather(row_delta, 'seq', axis=0, tiled=True)]
    pallas_call x0 -> x1, Pallas kernels: none -> 58.2 us  [body(): pl.pallas_call(functools.partial(kernel, X, Y, H), out_shape=(out, out, o...]
    all_gather x2 -> x0, waiting for transfers between devices: 52.6 us -> none  [the longest x1 52.6 us: body(): lax.all_gather(own_queries, 'seq', axis=0, tiled=True)]
  transfers between devices with their start and end apart: 6 -> 0, of which waited for: 4 -> 0; matrix products, arithmetic and copies ran while one was open for 1% -> 0% of each run, Pallas kernels for 0% -> 0%
where the time goes in v1:
time: 66.2 us; the launch traced here: 65.9 us
  Pallas kernels  58.2 us (88%)
  local copies, waits for them, and re-layouts  6.38 us (10%)
  between operations  1.33 us (2%)
    pallas_call x1, Pallas kernels, body(): pl.pallas_call(functools.partial(kernel, X, Y, H), out_shape=(out, out, o...  58.2 us
    unnamed x15, local copies, waits for them, and re-layouts  6.38 us

profile of v1, /device:TPU:1, one launch (start us, length us, event | category | flops | bytes accessed | tf_op | source)
XLA Modules:
  0.0 65.9 jit_solution(56912593013269305)
XLA Ops:
  0.6 0.0 copy-start.5
  1.3 0.0 copy-done.5
  1.3 0.0 copy-start
  1.3 0.9 %copy-done = bf16[128,384]{1,0:T(8,128)(2,1)S(1)} copy-done((bf16[128,384]{1,0:T(8,128)(2,1)S(1)}, bf16[128,384]{1,0:T(8,128)(2,1)}, u32[]{:S(2)}) %copy-start) | copy-done | bytes 98328
  2.2 0.0 copy-start.1
  2.2 0.9 %copy-done.1 = bf16[128,384]{1,0:T(8,128)(2,1)S(1)} copy-done((bf16[128,384]{1,0:T(8,128)(2,1)S(1)}, bf16[128,384]{1,0:T(8,128)(2,1)}, u32[]{:S(2)}) %copy-start.1) | copy-done | bytes 98328
  3.1 0.0 copy-start.2
  3.1 0.9 %copy-done.2 = bf16[128,384]{1,0:T(8,128)(2,1)S(1)} copy-done((bf16[128,384]{1,0:T(8,128)(2,1)S(1)}, bf16[128,384]{1,0:T(8,128)(2,1)}, u32[]{:S(2)}) %copy-start.2) | copy-done | bytes 98328
  4.0 0.0 copy-start.3
  4.0 0.9 %copy-done.3 = bf16[128,384]{1,0:T(8,128)(2,1)S(1)} copy-done((bf16[128,384]{1,0:T(8,128)(2,1)S(1)}, bf16[128,384]{1,0:T(8,128)(2,1)}, u32[]{:S(2)}) %copy-start.3) | copy-done | bytes 98328
  4.9 0.0 copy-start.4
  4.9 0.9 %copy-done.4 = bf16[128,384]{1,0:T(8,128)(2,1)S(1)} copy-done((bf16[128,384]{1,0:T(8,128)(2,1)S(1)}, bf16[128,384]{1,0:T(8,128)(2,1)}, u32[]{:S(2)}) %copy-start.4) | copy-done | bytes 98328
  5.8 58.2 %shard_map.94 = (bf16[32,1536]{1,0:T(8,128)(2,1)S(1)}, bf16[32,1536]{1,0:T(8,128)(2,1)S(1)}, bf16[32,1536]{1,0:T(8,128)(2,1)S(1)}) custom-call(s32[1,4]{1,0:T(1,128)S(1)} %copy-done.5, s32[1]{0:T(128)S(6)} %copy.13.vc_ref, bf16[128,384]{1,0:T(8,128)(2,1)S(1)} %copy-done, bf16[128,384]{1,0:T(8,128)(2,1)S(1)} %copy-done.1, bf16[128,384]{1,0:T(8,128)(2,1)S(1)} %copy-done.2, ...), custom_call_target="tpu_custom_call" | custom-call | tf_op jit(solution)/shard_map/pallas_call | solution.py:343
  64.0 0.6 copy.14
  64.6 0.6 copy.15
  65.3 0.6 copy.16
Async XLA Ops:
  0.6 0.7 %copy-start.5 = (s32[1,4]{1,0:T(1,128)S(1)}, s32[1,4]{1,0:T(1,128)}, u32[]{:S(2)}) copy-start(s32[1,4]{1,0:T(1,128)} %bi_ref.1) | copy-start | bytes 52
  1.3 0.9 %copy-start = (bf16[128,384]{1,0:T(8,128)(2,1)S(1)}, bf16[128,384]{1,0:T(8,128)(2,1)}, u32[]{:S(2)}) copy-start(bf16[128,384]{1,0:T(8,128)(2,1)} %q_ref.1) | copy-start | bytes 294916
  2.2 0.9 %copy-start.1 = (bf16[128,384]{1,0:T(8,128)(2,1)S(1)}, bf16[128,384]{1,0:T(8,128)(2,1)}, u32[]{:S(2)}) copy-start(bf16[128,384]{1,0:T(8,128)(2,1)} %k_ref.1) | copy-start | bytes 294916
  3.1 0.9 %copy-start.2 = (bf16[128,384]{1,0:T(8,128)(2,1)S(1)}, bf16[128,384]{1,0:T(8,128)(2,1)}, u32[]{:S(2)}) copy-start(bf16[128,384]{1,0:T(8,128)(2,1)} %v_ref.1) | copy-start | bytes 294916
  4.0 0.9 %copy-start.3 = (bf16[128,384]{1,0:T(8,128)(2,1)S(1)}, bf16[128,384]{1,0:T(8,128)(2,1)}, u32[]{:S(2)}) copy-start(bf16[128,384]{1,0:T(8,128)(2,1)} %o_ref.1) | copy-start | bytes 294916
  4.9 0.9 %copy-start.4 = (bf16[128,384]{1,0:T(8,128)(2,1)S(1)}, bf16[128,384]{1,0:T(8,128)(2,1)}, u32[]{:S(2)}) copy-start(bf16[128,384]{1,0:T(8,128)(2,1)} %g_ref.1) | copy-start | bytes 294916

commit v2 on v1

v2 whole, which is shorter than its diff:
```python
import functools

import jax
import jax.numpy as jnp
from jax import lax
from jax.experimental import pallas as pl
from jax.experimental.pallas import tpu as pltpu
from jax.sharding import PartitionSpec as P

HD = 128
BLK = 4
MB_DEV = 4
HL = 3
FEAT = HL * HD
SLOTS = MB_DEV * BLK
TOK = 128
WIDE = FEAT + HD
KEYS = 4 * TOK
SCALE = HD ** (-0.5)
LOG2E = 1.4426950408889634
MESH = pl.DeviceIdType.MESH
NT = (((1,), (1,)), ((), ()))
NN = (((1,), (0,)), ((), ()))


def mm(a, b, dims):
    return lax.dot_general(a, b, dims, preferred_element_type=jnp.float32)


def cols(hh):
    return slice(hh * HD, (hh + 1) * HD)


def kernel(
    X, Y, H,
    bi_ref, vc_ref, q_hbm, k_ref, v_ref, o_hbm, g_hbm,
    gq_ref, gk_ref, gv_ref,
    q_ref, o_ref, g_ref,
    qbuf, gbuf, kbuf, vbuf, kt, ebuf, dbuf, dqt, mrow, frow, fxrow, srow, srow2, sxb, syb,
    dqs, rxb, dqo, dys, ryb, dqf, gpart, crecv, fsend, frecv,
    ysend, yrecv, xsend, xrecv, kvsend, kvrecv, ssx, srx, ssy, sry,
    dxs, dxr, dss, dsr, css, csr, fss, fsr, hss, hsr, lsem,
):
    C = Y * SLOTS
    s = lax.axis_index("seq")
    h = lax.axis_index("head")
    c = lax.rem(s, 2)
    x = lax.rem(s // 2, X)
    y = lax.rem(s // (2 * X), Y)
    z = s // (2 * X * Y)

    def dev(z_, y_, x_, c_, h_):
        return {"seq": ((z_ * Y + y_) * X + x_) * 2 + c_, "head": h_}

    def up(v, d, n):
        return lax.rem(v + d, n)

    def dn(v, d, n):
        return lax.rem(v + n - d, n)

    quad = [(0, 1), (1, 0), (1, 1)]
    final = [(dz, dh) for dz in range(2) for dh in range(H) if dz or dh]
    xp = [dev(z, y, up(x, e, X), c, h) for e in range(1, X)]
    yp = [dev(z, up(y, d, Y), x, c, h) for d in range(1, Y)]
    qp = [dev(up(z, dz, 2), y, x, up(c, dc, 2), h) for dz, dc in quad]
    fp = [dev(up(z, dz, 2), y, x, c, up(h, dh, H)) for dz, dh in final]
    extra = [p for p, (dz, dh) in zip(fp, final) if dh]

    barrier = pltpu.get_barrier_semaphore()
    greet = xp + yp + qp + extra
    for p in greet:
        pl.semaphore_signal(barrier, inc=1, device_id=p, device_id_type=MESH)

    local = [
        pltpu.make_async_copy(a, b, lsem.at[i])
        for i, (a, b) in enumerate((
            (q_hbm, q_ref), (g_hbm, g_ref), (o_hbm, o_ref), (k_ref, kbuf.at[0]), (v_ref, vbuf.at[0]),
        ))
    ]
    for cp in local:
        cp.start()

    def rcopy(src, dst, ss, rs, to):
        return pltpu.make_async_remote_copy(
            src_ref=src, dst_ref=dst, send_sem=ss, recv_sem=rs,
            device_id=to, device_id_type=MESH,
        )

    count = vc_ref[0] * BLK
    b = [bi_ref[0, j] * BLK for j in range(MB_DEV)]

    def targets(idx):
        j = idx // BLK
        t = jnp.where(j == 0, b[0], jnp.where(j == 1, b[1], jnp.where(j == 2, b[2], b[3])))
        return jnp.where(idx < count, t + lax.rem(idx, BLK), -1)

    ri = lax.broadcasted_iota(jnp.int32, (SLOTS, TOK), 0)
    li = lax.broadcasted_iota(jnp.int32, (SLOTS, TOK), 1)
    sel = jnp.where(targets(ri) == li, 1.0, 0.0).astype(jnp.bfloat16)
    local[0].wait()
    qbuf[0, 0] = mm(sel, q_ref[...], NN).astype(jnp.bfloat16)
    pl.semaphore_wait(barrier, len(greet))

    near = [t for i in range(1, (Y + 1) // 2) for t in (i, Y - i)]
    xorder = ([2] if X > 2 else []) + [e for e in range(1, X) if e != 2]
    sent = []

    def begin(cp):
        cp.start()
        sent.append(cp)
        return cp

    def ycopy(i, d):
        buf = (qbuf, gbuf)[i]
        return rcopy(buf.at[0, 0], buf.at[0, d], ysend.at[i, d - 1], yrecv.at[i, d - 1], yp[d - 1])

    def xcopy(i, d, e):
        buf = (qbuf, gbuf)[i]
        return rcopy(buf.at[0, d], buf.at[e, d], xsend.at[i, d, e - 1], xrecv.at[i, d, e - 1], xp[e - 1])

    def kvcopy(i, j):
        src, buf = ((k_ref, kbuf), (v_ref, vbuf))[i]
        return rcopy(src, buf.at[j + 1], kvsend.at[i, j], kvrecv.at[i, j], qp[j])

    def forward(i, d):
        if d:
            ycopy(i, d).wait_recv()
        for e in xorder:
            begin(xcopy(i, d, e))

    for d in [Y // 2] + near:
        begin(ycopy(0, d))
    for e in xorder:
        begin(xcopy(0, 0, e))
    for j in (1, 2, 0):
        begin(kvcopy(0, j))
    local[1].wait()
    local[2].wait()
    own_g = mm(sel, g_ref[...], NN)
    prod = own_g * mm(sel, o_ref[...], NN)
    dcol = jnp.zeros((SLOTS, HD), jnp.float32)
    for hh in range(HL):
        dcol = jnp.where(li == hh, jnp.sum(prod[:, cols(hh)], axis=1, keepdims=True), dcol)
    gbuf[0, 0] = jnp.concatenate([own_g.astype(jnp.bfloat16), dcol.astype(jnp.bfloat16)], axis=1)
    for d in [Y // 2] + near:
        begin(ycopy(1, d))
    for j in (1, 2, 0):
        begin(kvcopy(1, j))
    order = near + [Y // 2]
    for d in order:
        forward(0, d)

    local[3].wait()
    for j in range(3):
        kvcopy(0, j).wait_recv()
    for hh in range(HL):
        kt[hh] = kbuf[:, :, cols(hh)].reshape(KEYS, HD).T

    mrow[...] = jnp.zeros_like(mrow)
    srow[...] = jnp.zeros_like(srow)
    arrive = [e for e in range(1, X) if e != 2] + ([2] if X > 2 else [])

    def score(e):
        for hh in range(HL):
            kh = kbuf[:, :, cols(hh)].reshape(KEYS, HD)
            qh = qbuf[e, :, :, cols(hh)].reshape(C, HD)
            s2 = mm(kh, qh, NT) * (SCALE * LOG2E)
            m = jnp.max(s2, axis=0, keepdims=True)
            ex = jnp.exp2(s2 - m)
            tot = jnp.sum(ex, axis=0, keepdims=True)
            ebuf[e, hh] = ex
            n = e * HL + hh
            mrow[n : n + 1, :] = m
            srow[n : n + 1, :] = m + jnp.log2(tot)

    def combine(parts):
        top = functools.reduce(jnp.maximum, parts)
        return top + jnp.log2(sum(jnp.exp2(p - top) for p in parts))

    score(0)
    for d in [0] + order:
        forward(1, d)
    for e in arrive:
        for d in [0] + order:
            xcopy(0, d, e).wait_recv()
        score(e)
    stat_x = [
        begin(rcopy(srow, sxb.at[e - 1], ssx.at[e - 1], srx.at[e - 1], xp[e - 1]))
        for e in range(1, X)
    ]

    def dprobs(e):
        for hh in range(HL):
            vh = vbuf[:, :, cols(hh)].reshape(KEYS, HD)
            lane = lax.broadcasted_iota(jnp.int32, (KEYS, HD), 1)
            neg = jnp.where(lane == hh, -1.0, 0.0).astype(jnp.bfloat16)
            gh = gbuf[e, :, :, cols(hh)].reshape(C, HD)
            dh = gbuf[e, :, :, FEAT:WIDE].reshape(C, HD)
            dp = mm(jnp.concatenate([vh, neg], 1), jnp.concatenate([gh, dh], 1), NT)
            dd = ebuf[e, hh] * dp
            dbuf[e, hh] = dd
            dqt[e, hh] = mm(kt[hh], dd.astype(jnp.bfloat16), NN)

    local[4].wait()
    for j in range(3):
        kvcopy(1, j).wait_recv()
    dprobs(0)
    for cp in stat_x:
        cp.wait_recv()
    srow2[...] = srow[...]
    for i in range(X):
        parts = [srow[i * HL : (i + 1) * HL, :]]
        for e in range(1, X):
            n = (i - e) % X * HL
            parts.append(sxb[e - 1, n : n + HL, :])
        srow2[i * HL : (i + 1) * HL, :] = combine(parts)
    stat_y = [
        begin(rcopy(srow2, syb.at[d - 1], ssy.at[d - 1], sry.at[d - 1], yp[d - 1]))
        for d in [Y // 2] + near
    ]
    fxrow[...] = jnp.exp2(mrow[...] - srow2[...])

    def scaled(e, hh):
        n = e * HL + hh
        return (dqt[e, hh] * (fxrow[n : n + 1, :] * SCALE)).T

    dq_x = []
    for e in arrive:
        for d in [0] + order:
            xcopy(1, d, e).wait_recv()
        dprobs(e)
        for hh in range(HL):
            dqs[e - 1, :, cols(hh)] = scaled(e, hh).astype(jnp.bfloat16)
        dq_x.append(
            begin(rcopy(dqs.at[e - 1], rxb.at[e - 1], dxs.at[e - 1], dxr.at[e - 1], xp[X - e - 1]))
        )
    for hh in range(HL):
        dqo[:, cols(hh)] = scaled(0, hh)
    for cp in stat_y:
        cp.wait_recv()
    parts = [srow2[...]] + [pltpu.roll(syb[d - 1], d * SLOTS, 1) for d in range(1, Y)]
    log_total = combine(parts)
    frow[...] = jnp.exp2(mrow[...] - log_total)
    fyt = jnp.exp2(srow2[...] - log_total).T

    core = dev(z, y, x, 1 - c, h)

    def grads(hh):
        f = [frow[i * HL + hh : i * HL + hh + 1, :] for i in range(X)]
        w = jnp.concatenate([(ebuf[i, hh] * f[i]).astype(jnp.bfloat16) for i in range(X)], axis=1)
        gvp = mm(w, gbuf[:, :, :, cols(hh)].reshape(X * C, HD), NN)
        ds = jnp.concatenate([(dbuf[i, hh] * f[i]).astype(jnp.bfloat16) for i in range(X)], axis=1)
        gkp = mm(ds, qbuf[:, :, :, cols(hh)].reshape(X * C, HD), NN) * SCALE
        for a, val in enumerate((gkp, gvp)):
            for i in range(4):
                gpart[hh, i % 2, a, i // 2] = val[i * TOK : (i + 1) * TOK].astype(jnp.bfloat16)
        return begin(rcopy(gpart.at[hh, 1], crecv.at[hh], css.at[hh], csr.at[hh], core))

    def spread(hh, cp):
        cp.wait_recv()
        for a in range(2):
            for i in range(2):
                tot = gpart[hh, 0, a, i].astype(jnp.float32) + crecv[hh, a, i].astype(jnp.float32)
                fsend[hh, i, :, a] = tot.astype(jnp.bfloat16).reshape(H, TOK // H, HD)
        for n, (dz, dh) in enumerate(final):
            begin(rcopy(
                fsend.at[hh, dz, up(h, dh, H)], frecv.at[hh, dz, h],
                fss.at[hh, n], fsr.at[hh, n], fp[n],
            ))
        frecv[hh, 0, h] = fsend[hh, 0, h]

    c0 = grads(0)
    c1 = grads(1)
    spread(0, c0)
    for cp in dq_x:
        cp.wait_recv()
    for hh in range(HL):
        tot = dqo[:, cols(hh)]
        for e in range(1, X):
            tot = tot + rxb[e - 1, :, cols(hh)].astype(jnp.float32)
        tot = (tot * fyt[:, hh : hh + 1]).astype(jnp.bfloat16)
        dys[:, :, cols(hh)] = tot.reshape(Y, SLOTS, HD)
    dq_y = [
        begin(rcopy(dys.at[d], ryb.at[d - 1], dss.at[d - 1], dsr.at[d - 1], yp[Y - d - 1]))
        for d in [Y // 2] + near
    ]
    spread(1, c1)
    c2 = grads(2)
    spread(2, c2)
    for cp in dq_y:
        cp.wait_recv()
    tot = dys[0].astype(jnp.float32)
    for d in range(1, Y):
        tot = tot + ryb[d - 1].astype(jnp.float32)
    dqf[h] = tot.astype(jnp.bfloat16)
    for dh in range(1, H):
        to = dev(z, y, x, c, up(h, dh, H))
        begin(rcopy(dqf.at[h], dqf.at[h], hss.at[dh - 1], hsr.at[dh - 1], to))

    for hh in range(HL):
        for n, (dz, dh) in enumerate(final):
            rcopy(
                fsend.at[hh, 0, 0], frecv.at[hh, dz, dn(h, dh, H)],
                fss.at[hh, n], fsr.at[hh, n], fp[n],
            ).wait_recv()
        for i in range(H):
            lanes = slice(i * FEAT + hh * HD, i * FEAT + (hh + 1) * HD)
            for a, ref in enumerate((gk_ref, gv_ref)):
                both = frecv[hh, 0, i, a].astype(jnp.float32) + frecv[hh, 1, i, a].astype(jnp.float32)
                ref[:, lanes] = both.astype(jnp.bfloat16)
    for dh in range(1, H):
        slot = dn(h, dh, H)
        rcopy(dqf.at[slot], dqf.at[slot], hss.at[dh - 1], hsr.at[dh - 1], xp[0]).wait_recv()
    out_rows = TOK // H
    pr = lax.broadcasted_iota(jnp.int32, (out_rows, SLOTS), 0) + h * out_rows
    pj = lax.broadcasted_iota(jnp.int32, (out_rows, SLOTS), 1)
    put = jnp.where(targets(pj) == pr, 1.0, 0.0).astype(jnp.bfloat16)
    for i in range(H):
        gq_ref[:, i * FEAT : (i + 1) * FEAT] = mm(put, dqf[i], NN).astype(jnp.bfloat16)
    for cp in sent:
        cp.wait_send()


def body(X, Y, H, queries, key_states, value_states, attn_output, grad_output, block_index, valid_count):
    C = Y * SLOTS
    bf, f32 = jnp.bfloat16, jnp.float32
    V = pltpu.VMEM
    D = pltpu.SemaphoreType.DMA
    nf = 2 * H - 1
    scratch = [
        V((TOK, FEAT), bf),
        V((TOK, FEAT), bf),
        V((TOK, FEAT), bf),
        V((X, Y, SLOTS, FEAT), bf),
        V((X, Y, SLOTS, WIDE), bf),
        V((4, TOK, FEAT), bf),
        V((4, TOK, FEAT), bf),
        V((HL, HD, KEYS), bf),
        V((X, HL, KEYS, C), f32),
        V((X, HL, KEYS, C), f32),
        V((X, HL, HD, C), f32),
        V((16, C), f32),
        V((16, C), f32),
        V((16, C), f32),
        V((16, C), f32),
        V((16, C), f32),
        V((X - 1, 16, C), f32),
        V((Y - 1, 16, C), f32),
        V((X - 1, C, FEAT), bf),
        V((X - 1, C, FEAT), bf),
        V((C, FEAT), f32),
        V((Y, SLOTS, FEAT), bf),
        V((Y - 1, SLOTS, FEAT), bf),
        V((H, SLOTS, FEAT), bf),
        V((HL, 2, 2, 2, TOK, HD), bf),
        V((HL, 2, 2, TOK, HD), bf),
        V((HL, 2, H, 2, TOK // H, HD), bf),
        V((HL, 2, H, 2, TOK // H, HD), bf),
        D((2, Y - 1)), D((2, Y - 1)),
        D((2, Y, X - 1)), D((2, Y, X - 1)),
        D((2, 3)), D((2, 3)),
        D((X - 1,)), D((X - 1,)),
        D((Y - 1,)), D((Y - 1,)),
        D((X - 1,)), D((X - 1,)),
        D((Y - 1,)), D((Y - 1,)),
        D((HL,)), D((HL,)),
        D((HL, nf)), D((HL, nf)),
        D((H - 1,)), D((H - 1,)),
        D((5,)),
    ]
    out = jax.ShapeDtypeStruct((TOK // H, H * FEAT), bf)
    vm = pl.BlockSpec(memory_space=pltpu.VMEM)
    hb = pl.BlockSpec(memory_space=pltpu.HBM)
    sm = pl.BlockSpec(memory_space=pltpu.SMEM)
    return pl.pallas_call(
        functools.partial(kernel, X, Y, H),
        out_shape=(out, out, out),
        in_specs=[sm, sm, hb, hb, hb, hb, hb],
        out_specs=(vm, vm, vm),
        scratch_shapes=scratch,
        compiler_params=pltpu.CompilerParams(
            collective_id=0, has_side_effects=True, vmem_limit_bytes=63 * 1024 * 1024
        ),
    )(block_index, valid_count, queries, key_states, value_states, attn_output, grad_output)


def build(mesh, X, Y):
    H = mesh.shape["head"]
    in_specs = tuple([P("seq", "head")] * 5) + (P("seq", None), P("seq"))
    out_specs = tuple([P(("seq", "head"), None)] * 3)
    return jax.shard_map(
        functools.partial(body, X, Y, H),
        mesh=mesh, in_specs=in_specs, out_specs=out_specs, check_vma=False,
    )


def solution(mesh):
    return build(mesh, 4, 8)
```

time: 66.2 us -> 57.9 us (0.87)
  Pallas kernels: 58.2 us -> 53.3 us
  local copies, waits for them, and re-layouts: 6.38 us -> 3.15 us
    pallas_call x1, Pallas kernels: 58.2 us -> 53.3 us  [body(): pl.pallas_call(functools.partial(kernel, X, Y, H), out_shape=(out, out, o...]
    unnamed x15 -> x7, local copies, waits for them, and re-layouts: 6.38 us -> 3.15 us
where the time goes in v2:
time: 57.9 us; the launch traced here: 57.7 us
  Pallas kernels  53.3 us (92%)
  local copies, waits for them, and re-layouts  3.15 us (5%)
  between operations  1.3 us (2%)
    pallas_call x1, Pallas kernels, body(): pl.pallas_call(functools.partial(kernel, X, Y, H), out_shape=(out, out, o...  53.3 us
    unnamed x7, local copies, waits for them, and re-layouts  3.15 us

profile of v2, /device:TPU:1, one launch (start us, length us, event | category | flops | bytes accessed | tf_op | source)
XLA Modules:
  0.0 57.7 jit_solution(15218362662379043011)
XLA Ops:
  1.3 53.3 %shard_map.94 = (bf16[32,1536]{1,0:T(8,128)(2,1)}, bf16[32,1536]{1,0:T(8,128)(2,1)}, bf16[32,1536]{1,0:T(8,128)(2,1)}) custom-call(s32[1,4]{1,0:T(1,128)} %bi_ref.1, s32[1]{0:T(128)S(6)} %copy.13.vc_ref, bf16[128,384]{1,0:T(8,128)(2,1)} %q_hbm.1, bf16[128,384]{1,0:T(8,128)(2,1)} %k_ref.1, bf16[128,384]{1,0:T(8,128)(2,1)} %v_ref.1, bf16[128,384]{1,0:T(8,128)(2,1)} %o_hbm.1, ...), custom_call_target="tpu_custom_call" | custom-call | tf_op jit(solution)/shard_map/pallas_call | solution.py:375
  54.6 0.0 copy-start.1
  54.6 1.6 %copy.14 = bf16[32,1536]{1,0:T(8,128)(2,1)} copy(bf16[32,1536]{1,0:T(8,128)(2,1)} %get-tuple-element.6) | data formatting | bytes 196608
  56.1 0.0 copy-done.1
  56.1 0.0 copy-start
  56.1 0.6 %copy.15 = bf16[32,1536]{1,0:T(8,128)(2,1)} copy(bf16[32,1536]{1,0:T(8,128)(2,1)S(1)} %copy-done.1) | data formatting | bytes 196608
  56.8 0.3 copy-done
  57.1 0.6 %copy.16 = bf16[32,1536]{1,0:T(8,128)(2,1)} copy(bf16[32,1536]{1,0:T(8,128)(2,1)S(1)} %copy-done) | data formatting | bytes 196608
Async XLA Ops:
  54.6 1.6 %copy-start.1 = (bf16[32,1536]{1,0:T(8,128)(2,1)S(1)}, bf16[32,1536]{1,0:T(8,128)(2,1)}, u32[]{:S(2)}) copy-start(bf16[32,1536]{1,0:T(8,128)(2,1)} %get-tuple-element.7) | copy-start | bytes 294916
  56.1 0.9 %copy-start = (bf16[32,1536]{1,0:T(8,128)(2,1)S(1)}, bf16[32,1536]{1,0:T(8,128)(2,1)}, u32[]{:S(2)}) copy-start(bf16[32,1536]{1,0:T(8,128)(2,1)} %get-tuple-element.8) | copy-start | bytes 294916

commit v3 on v2

--- a/solution.py
+++ b/solution.py
@@ -34,11 +34,11 @@
 def kernel(
     X, Y, H,
     bi_ref, vc_ref, q_hbm, k_ref, v_ref, o_hbm, g_hbm,
-    gq_ref, gk_ref, gv_ref,
+    parts_ref,
     q_ref, o_ref, g_ref,
-    qbuf, gbuf, kbuf, vbuf, kt, ebuf, dbuf, dqt, mrow, frow, fxrow, srow, srow2, sxb, syb,
+    qbuf, gbuf, kbuf, vbuf, kt, ebuf, dbuf, dqt, mrow, frow, wrow, srow, srow2, sxb, sxl, syb,
     dqs, rxb, dqo, dys, ryb, dqf, gpart, crecv, fsend, frecv,
-    ysend, yrecv, xsend, xrecv, kvsend, kvrecv, ssx, srx, ssy, sry,
+    ysend, yrecv, xsend, xrecv, kvsend, kvrecv, ssx, srx, slx, rlx, ssy, sry,
     dxs, dxr, dss, dsr, css, csr, fss, fsr, hss, hsr, lsem,
 ):
     C = Y * SLOTS
@@ -121,12 +121,6 @@
     def kvcopy(i, j):
         src, buf = ((k_ref, kbuf), (v_ref, vbuf))[i]
         return rcopy(src, buf.at[j + 1], kvsend.at[i, j], kvrecv.at[i, j], qp[j])
-
-    def forward(i, d):
-        if d:
-            ycopy(i, d).wait_recv()
-        for e in xorder:
-            begin(xcopy(i, d, e))
 
     for d in [Y // 2] + near:
         begin(ycopy(0, d))
@@ -148,7 +142,14 @@
         begin(kvcopy(1, j))
     order = near + [Y // 2]
     for d in order:
-        forward(0, d)
+        ycopy(0, d).wait_recv()
+        for e in xorder:
+            begin(xcopy(0, d, e))
+    for e in xorder:
+        for d in [0] + order:
+            if d and e == xorder[0]:
+                ycopy(1, d).wait_recv()
+            begin(xcopy(1, d, e))
 
     local[3].wait()
     for j in range(3):
@@ -178,14 +179,16 @@
         return top + jnp.log2(sum(jnp.exp2(p - top) for p in parts))
 
     score(0)
-    for d in [0] + order:
-        forward(1, d)
     for e in arrive:
         for d in [0] + order:
             xcopy(0, d, e).wait_recv()
         score(e)
-    stat_x = [
-        begin(rcopy(srow, sxb.at[e - 1], ssx.at[e - 1], srx.at[e - 1], xp[e - 1]))
+    stat_y = [
+        begin(rcopy(srow, syb.at[d - 1], ssy.at[d - 1], sry.at[d - 1], yp[d - 1]))
+        for d in [Y // 2] + near
+    ]
+    stat_l = [
+        begin(rcopy(srow, sxl.at[e - 1], slx.at[e - 1], rlx.at[e - 1], xp[e - 1]))
         for e in range(1, X)
     ]
 
@@ -204,28 +207,14 @@
     local[4].wait()
     for j in range(3):
         kvcopy(1, j).wait_recv()
-    dprobs(0)
-    for cp in stat_x:
-        cp.wait_recv()
-    srow2[...] = srow[...]
-    for i in range(X):
-        parts = [srow[i * HL : (i + 1) * HL, :]]
-        for e in range(1, X):
-            n = (i - e) % X * HL
-            parts.append(sxb[e - 1, n : n + HL, :])
-        srow2[i * HL : (i + 1) * HL, :] = combine(parts)
-    stat_y = [
-        begin(rcopy(srow2, syb.at[d - 1], ssy.at[d - 1], sry.at[d - 1], yp[d - 1]))
-        for d in [Y // 2] + near
-    ]
-    fxrow[...] = jnp.exp2(mrow[...] - srow2[...])
 
     def scaled(e, hh):
         n = e * HL + hh
-        return (dqt[e, hh] * (fxrow[n : n + 1, :] * SCALE)).T
+        row = jnp.exp2(mrow[n : n + 1, :] - srow[n : n + 1, :])
+        return (dqt[e, hh] * (row * SCALE)).T
 
     dq_x = []
-    for e in arrive:
+    def send_dq(e):
         for d in [0] + order:
             xcopy(1, d, e).wait_recv()
         dprobs(e)
@@ -234,14 +223,36 @@
         dq_x.append(
             begin(rcopy(dqs.at[e - 1], rxb.at[e - 1], dxs.at[e - 1], dxr.at[e - 1], xp[X - e - 1]))
         )
+    send_dq(xorder[0])
+    dprobs(0)
     for hh in range(HL):
         dqo[:, cols(hh)] = scaled(0, hh)
+
     for cp in stat_y:
         cp.wait_recv()
-    parts = [srow2[...]] + [pltpu.roll(syb[d - 1], d * SLOTS, 1) for d in range(1, Y)]
-    log_total = combine(parts)
-    frow[...] = jnp.exp2(mrow[...] - log_total)
-    fyt = jnp.exp2(srow2[...] - log_total).T
+    srow2[...] = combine([srow[...]] + [pltpu.roll(syb[d - 1], d * SLOTS, 1) for d in range(1, Y)])
+    stat_x = [
+        begin(rcopy(srow2, sxb.at[e - 1], ssx.at[e - 1], srx.at[e - 1], xp[e - 1]))
+        for e in xorder
+    ]
+    for e in xorder[1:]:
+        send_dq(e)
+    for cp in stat_x + stat_l:
+        cp.wait_recv()
+    for i in range(X):
+        rows = slice(i * HL, (i + 1) * HL)
+        parts = [srow2[rows, :]]
+        for e in range(1, X):
+            n = (i - e) % X * HL
+            parts.append(sxb[e - 1, n : n + HL, :])
+        log_total = combine(parts)
+        frow[rows, :] = jnp.exp2(mrow[rows, :] - log_total)
+        if i == 0:
+            wrow[...] = jnp.zeros_like(wrow)
+            wrow[rows, :] = jnp.exp2(srow[rows, :] - log_total)
+            for e in range(1, X):
+                n = e * HL
+                wrow[n : n + HL, :] = jnp.exp2(sxl[X - e - 1, n : n + HL, :] - log_total)
 
     core = dev(z, y, x, 1 - c, h)
 
@@ -272,14 +283,15 @@
     c0 = grads(0)
     c1 = grads(1)
     spread(0, c0)
+    weight = wrow[...].T
     for cp in dq_x:
         cp.wait_recv()
     for hh in range(HL):
-        tot = dqo[:, cols(hh)]
+        tot = dqo[:, cols(hh)] * weight[:, hh : hh + 1]
         for e in range(1, X):
-            tot = tot + rxb[e - 1, :, cols(hh)].astype(jnp.float32)
-        tot = (tot * fyt[:, hh : hh + 1]).astype(jnp.bfloat16)
-        dys[:, :, cols(hh)] = tot.reshape(Y, SLOTS, HD)
+            n = e * HL + hh
+            tot = tot + rxb[e - 1, :, cols(hh)].astype(jnp.float32) * weight[:, n : n + 1]
+        dys[:, :, cols(hh)] = tot.astype(jnp.bfloat16).reshape(Y, SLOTS, HD)
     dq_y = [
         begin(rcopy(dys.at[d], ryb.at[d - 1], dss.at[d - 1], dsr.at[d - 1], yp[Y - d - 1]))
         for d in [Y // 2] + near
@@ -305,9 +317,9 @@
             ).wait_recv()
         for i in range(H):
             lanes = slice(i * FEAT + hh * HD, i * FEAT + (hh + 1) * HD)
-            for a, ref in enumerate((gk_ref, gv_ref)):
-                both = frecv[hh, 0, i, a].astype(jnp.float32) + frecv[hh, 1, i, a].astype(jnp.float32)
-                ref[:, lanes] = both.astype(jnp.bfloat16)
+            for a in range(2):
+                for p in range(2):
+                    parts_ref[p, a + 1, :, lanes] = frecv[hh, p, i, a]
     for dh in range(1, H):
         slot = dn(h, dh, H)
         rcopy(dqf.at[slot], dqf.at[slot], hss.at[dh - 1], hsr.at[dh - 1], xp[0]).wait_recv()
@@ -316,7 +328,10 @@
     pj = lax.broadcasted_iota(jnp.int32, (out_rows, SLOTS), 1)
     put = jnp.where(targets(pj) == pr, 1.0, 0.0).astype(jnp.bfloat16)
     for i in range(H):
-        gq_ref[:, i * FEAT : (i + 1) * FEAT] = mm(put, dqf[i], NN).astype(jnp.bfloat16)
+        lanes = slice(i * FEAT, (i + 1) * FEAT)
+        for p in range(2):
+            half = jnp.where(pj // (SLOTS // 2) == p, put, jnp.zeros_like(put))
+            parts_ref[p, 0, :, lanes] = mm(half, dqf[i], NN).astype(jnp.bfloat16)
     for cp in sent:
         cp.wait_send()
 
@@ -345,6 +360,7 @@
         V((16, C), f32),
         V((16, C), f32),
         V((X - 1, 16, C), f32),
+        V((X - 1, 16, C), f32),
         V((Y - 1, 16, C), f32),
         V((X - 1, C, FEAT), bf),
         V((X - 1, C, FEAT), bf),
@@ -360,6 +376,7 @@
         D((2, Y, X - 1)), D((2, Y, X - 1)),
         D((2, 3)), D((2, 3)),
         D((X - 1,)), D((X - 1,)),
+        D((X - 1,)), D((X - 1,)),
         D((Y - 1,)), D((Y - 1,)),
         D((X - 1,)), D((X - 1,)),
         D((Y - 1,)), D((Y - 1,)),
@@ -369,19 +386,23 @@
         D((5,)),
     ]
     out = jax.ShapeDtypeStruct((TOK // H, H * FEAT), bf)
+    parts = jax.ShapeDtypeStruct((2, 3, TOK // H, H * FEAT), bf)
     vm = pl.BlockSpec(memory_space=pltpu.VMEM)
     hb = pl.BlockSpec(memory_space=pltpu.HBM)
     sm = pl.BlockSpec(memory_space=pltpu.SMEM)
-    return pl.pallas_call(
+    parts = pl.pallas_call(
         functools.partial(kernel, X, Y, H),
-        out_shape=(out, out, out),
+        out_shape=parts,
         in_specs=[sm, sm, hb, hb, hb, hb, hb],
-        out_specs=(vm, vm, vm),
+        out_specs=vm,
         scratch_shapes=scratch,
         compiler_params=pltpu.CompilerParams(
             collective_id=0, has_side_effects=True, vmem_limit_bytes=63 * 1024 * 1024
         ),
     )(block_index, valid_count, queries, key_states, value_states, attn_output, grad_output)
+    return tuple(
+        (parts[0, a].astype(f32) + parts[1, a].astype(f32)).astype(bf) for a in range(3)
+    )
 
 
 def build(mesh, X, Y):

time: 57.9 us -> 55.8 us (0.964)
  local copies, waits for them, and re-layouts: 3.15 us -> 0 us
  other arithmetic: 0 us -> 1.87 us
  Pallas kernels: 53.3 us -> 52.5 us
    unnamed x7 -> x0, local copies, waits for them, and re-layouts: 3.15 us -> none
    convert_element_type x0 -> x1, other arithmetic: none -> 1.87 us  [body(): (parts[0, a].astype(f32) + parts[1, a].astype(f32)).astype(bf)]
    pallas_call x1, Pallas kernels: 53.3 us -> 52.5 us  [body(): pl.pallas_call(functools.partial(kernel, X, Y, H), out_shape=parts, in_sp...]
where the time goes in v3:
time: 55.8 us; the launch traced here: 55.6 us
  Pallas kernels  52.5 us (94%)
  other arithmetic  1.87 us (3%)
  between operations  1.29 us (2%)
    pallas_call x1, Pallas kernels, body(): pl.pallas_call(functools.partial(kernel, X, Y, H), out_shape=parts, in_sp...  52.5 us
    convert_element_type x1, other arithmetic, body(): (parts[0, a].astype(f32) + parts[1, a].astype(f32)).astype(bf)  1.87 us

profile of v3, /device:TPU:1, one launch (start us, length us, event | category | flops | bytes accessed | tf_op | source)
XLA Modules:
  0.0 55.6 jit_solution(4409770001250920652)
XLA Ops:
  1.3 52.5 %shard_map.94 = bf16[2,3,32,1536]{3,2,1,0:T(8,128)(2,1)} custom-call(s32[1,4]{1,0:T(1,128)} %bi_ref.1, s32[1]{0:T(128)S(6)} %copy.10.vc_ref, bf16[128,384]{1,0:T(8,128)(2,1)} %q_hbm.1, bf16[128,384]{1,0:T(8,128)(2,1)} %k_ref.1, bf16[128,384]{1,0:T(8,128)(2,1)} %v_ref.1, bf16[128,384]{1,0:T(8,128)(2,1)} %o_hbm.1, bf16[128,384]{1,0:T(8,128)(2,1)} %g_hbm.1), custom_call_target="tpu_custom_call" | custom-call | tf_op jit(solution)/shard_map/pallas_call | solution.py:393
  53.7 1.9 %fusion.2 = (bf16[32,1536]{1,0:T(8,128)(2,1)}, bf16[32,1536]{1,0:T(8,128)(2,1)}, bf16[32,1536]{1,0:T(8,128)(2,1)}) fusion(bf16[2,3,32,1536]{3,2,1,0:T(8,128)(2,1)} %shard_map.94), kind=kLoop, calls=%fused_computation.5 | loop fusion | flops 589824 | bytes 884736 | tf_op jit(solution)/shard_map/convert_element_type | solution.py:404

commit v4 on v3

--- a/solution.py
+++ b/solution.py
@@ -14,13 +14,13 @@
 FEAT = HL * HD
 SLOTS = MB_DEV * BLK
 TOK = 128
-WIDE = FEAT + HD
 KEYS = 4 * TOK
 SCALE = HD ** (-0.5)
 LOG2E = 1.4426950408889634
 MESH = pl.DeviceIdType.MESH
 NT = (((1,), (1,)), ((), ()))
 NN = (((1,), (0,)), ((), ()))
+TN = (((0,), (0,)), ((), ()))
 
 
 def mm(a, b, dims):
@@ -36,9 +36,9 @@
     bi_ref, vc_ref, q_hbm, k_ref, v_ref, o_hbm, g_hbm,
     parts_ref,
     q_ref, o_ref, g_ref,
-    qbuf, gbuf, kbuf, vbuf, kt, ebuf, dbuf, dqt, mrow, frow, wrow, srow, srow2, sxb, sxl, syb,
+    qbuf, gbuf, dly, dlx, kbuf, vbuf, kt, ebuf, dbuf, dqt, mrow, frow, wrow, srow, srow2, sxb, sxl, syb,
     dqs, rxb, dqo, dys, ryb, dqf, gpart, crecv, fsend, frecv,
-    ysend, yrecv, xsend, xrecv, kvsend, kvrecv, ssx, srx, slx, rlx, ssy, sry,
+    dysend, dyrecv, dxsend, dxrecv, ysend, yrecv, xsend, xrecv, kvsend, kvrecv, ssx, srx, slx, rlx, ssy, sry,
     dxs, dxr, dss, dsr, css, csr, fss, fsr, hss, hsr, lsem,
 ):
     C = Y * SLOTS
@@ -60,6 +60,7 @@
 
     quad = [(0, 1), (1, 0), (1, 1)]
     final = [(dz, dh) for dz in range(2) for dh in range(H) if dz or dh]
+    final.sort(key=lambda t: abs(t[1] - H // 2))
     xp = [dev(z, y, up(x, e, X), c, h) for e in range(1, X)]
     yp = [dev(z, up(y, d, Y), x, c, h) for d in range(1, Y)]
     qp = [dev(up(z, dz, 2), y, x, up(c, dc, 2), h) for dz, dc in quad]
@@ -135,9 +136,23 @@
     dcol = jnp.zeros((SLOTS, HD), jnp.float32)
     for hh in range(HL):
         dcol = jnp.where(li == hh, jnp.sum(prod[:, cols(hh)], axis=1, keepdims=True), dcol)
-    gbuf[0, 0] = jnp.concatenate([own_g.astype(jnp.bfloat16), dcol.astype(jnp.bfloat16)], axis=1)
+    gbuf[0, 0] = own_g.astype(jnp.bfloat16)
+    ident = jnp.where(
+        lax.broadcasted_iota(jnp.int32, (SLOTS, C), 0)
+        == lax.broadcasted_iota(jnp.int32, (SLOTS, C), 1), 1.0, 0.0,
+    ).astype(jnp.bfloat16)
+    dly[0] = mm(dcol.astype(jnp.bfloat16), ident, TN)[:8]
+
+    def dycopy(d):
+        return rcopy(dly.at[0], dly.at[d], dysend.at[d - 1], dyrecv.at[d - 1], yp[d - 1])
+
+    def dxcopy(e):
+        return rcopy(dlx.at[0], dlx.at[e], dxsend.at[e - 1], dxrecv.at[e - 1], xp[e - 1])
+
     for d in [Y // 2] + near:
         begin(ycopy(1, d))
+    for d in [Y // 2] + near:
+        begin(dycopy(d))
     for j in (1, 2, 0):
         begin(kvcopy(1, j))
     order = near + [Y // 2]
@@ -150,6 +165,11 @@
             if d and e == xorder[0]:
                 ycopy(1, d).wait_recv()
             begin(xcopy(1, d, e))
+    for d in order:
+        dycopy(d).wait_recv()
+    dlx[0] = sum([dly[0]] + [pltpu.roll(dly[d], d * SLOTS, 1) for d in range(1, Y)])
+    for e in xorder:
+        begin(dxcopy(e))
 
     local[3].wait()
     for j in range(3):
@@ -195,11 +215,8 @@
     def dprobs(e):
         for hh in range(HL):
             vh = vbuf[:, :, cols(hh)].reshape(KEYS, HD)
-            lane = lax.broadcasted_iota(jnp.int32, (KEYS, HD), 1)
-            neg = jnp.where(lane == hh, -1.0, 0.0).astype(jnp.bfloat16)
             gh = gbuf[e, :, :, cols(hh)].reshape(C, HD)
-            dh = gbuf[e, :, :, FEAT:WIDE].reshape(C, HD)
-            dp = mm(jnp.concatenate([vh, neg], 1), jnp.concatenate([gh, dh], 1), NT)
+            dp = mm(vh, gh, NT) - dlx[e, hh : hh + 1, :]
             dd = ebuf[e, hh] * dp
             dbuf[e, hh] = dd
             dqt[e, hh] = mm(kt[hh], dd.astype(jnp.bfloat16), NN)
@@ -214,19 +231,23 @@
         return (dqt[e, hh] * (row * SCALE)).T
 
     dq_x = []
-    def send_dq(e):
+    def make_dq(e):
         for d in [0] + order:
             xcopy(1, d, e).wait_recv()
+        dxcopy(e).wait_recv()
         dprobs(e)
         for hh in range(HL):
             dqs[e - 1, :, cols(hh)] = scaled(e, hh).astype(jnp.bfloat16)
+
+    def send_dq(e):
         dq_x.append(
             begin(rcopy(dqs.at[e - 1], rxb.at[e - 1], dxs.at[e - 1], dxr.at[e - 1], xp[X - e - 1]))
         )
-    send_dq(xorder[0])
+
     dprobs(0)
     for hh in range(HL):
         dqo[:, cols(hh)] = scaled(0, hh)
+    make_dq(xorder[0])
 
     for cp in stat_y:
         cp.wait_recv()
@@ -235,7 +256,9 @@
         begin(rcopy(srow2, sxb.at[e - 1], ssx.at[e - 1], srx.at[e - 1], xp[e - 1]))
         for e in xorder
     ]
+    send_dq(xorder[0])
     for e in xorder[1:]:
+        make_dq(e)
         send_dq(e)
     for cp in stat_x + stat_l:
         cp.wait_recv()
@@ -347,7 +370,9 @@
         V((TOK, FEAT), bf),
         V((TOK, FEAT), bf),
         V((X, Y, SLOTS, FEAT), bf),
-        V((X, Y, SLOTS, WIDE), bf),
+        V((X, Y, SLOTS, FEAT), bf),
+        V((Y, 8, C), f32),
+        V((X, 8, C), f32),
         V((4, TOK, FEAT), bf),
         V((4, TOK, FEAT), bf),
         V((HL, HD, KEYS), bf),
@@ -372,6 +397,8 @@
         V((HL, 2, 2, TOK, HD), bf),
         V((HL, 2, H, 2, TOK // H, HD), bf),
         V((HL, 2, H, 2, TOK // H, HD), bf),
+        D((Y - 1,)), D((Y - 1,)),
+        D((X - 1,)), D((X - 1,)),
         D((2, Y - 1)), D((2, Y - 1)),
         D((2, Y, X - 1)), D((2, Y, X - 1)),
         D((2, 3)), D((2, 3)),

time: 55.8 us -> 55.8 us (level)
  no operation moved by 1% of the time
where the time goes in v4:
time: 55.8 us; the launch traced here: 55.6 us
  Pallas kernels  52.4 us (94%)
  other arithmetic  1.87 us (3%)
  between operations  1.29 us (2%)
    pallas_call x1, Pallas kernels, body(): pl.pallas_call(functools.partial(kernel, X, Y, H), out_shape=parts, in_sp...  52.4 us
    convert_element_type x1, other arithmetic, body(): (parts[0, a].astype(f32) + parts[1, a].astype(f32)).astype(bf)  1.87 us

profile of v4, /device:TPU:1, one launch (start us, length us, event | category | flops | bytes accessed | tf_op | source)
XLA Modules:
  0.0 55.6 jit_solution(6767735382880018820)
XLA Ops:
  1.3 52.4 %shard_map.94 = bf16[2,3,32,1536]{3,2,1,0:T(8,128)(2,1)} custom-call(s32[1,4]{1,0:T(1,128)} %bi_ref.1, s32[1]{0:T(128)S(6)} %copy.10.vc_ref, bf16[128,384]{1,0:T(8,128)(2,1)} %q_hbm.1, bf16[128,384]{1,0:T(8,128)(2,1)} %k_ref.1, bf16[128,384]{1,0:T(8,128)(2,1)} %v_ref.1, bf16[128,384]{1,0:T(8,128)(2,1)} %o_hbm.1, bf16[128,384]{1,0:T(8,128)(2,1)} %g_hbm.1), custom_call_target="tpu_custom_call" | custom-call | tf_op jit(solution)/shard_map/pallas_call | solution.py:420
  53.7 1.9 %fusion.2 = (bf16[32,1536]{1,0:T(8,128)(2,1)}, bf16[32,1536]{1,0:T(8,128)(2,1)}, bf16[32,1536]{1,0:T(8,128)(2,1)}) fusion(bf16[2,3,32,1536]{3,2,1,0:T(8,128)(2,1)} %shard_map.94), kind=kLoop, calls=%fused_computation.5 | loop fusion | flops 589824 | bytes 884736 | tf_op jit(solution)/shard_map/convert_element_type | solution.py:431

commit v5 on v3

--- a/solution.py
+++ b/solution.py
@@ -280,6 +280,7 @@
             ))
         frecv[hh, 0, h] = fsend[hh, 0, h]
 
+    early = len(sent)
     c0 = grads(0)
     c1 = grads(1)
     spread(0, c0)
@@ -299,6 +300,8 @@
     spread(1, c1)
     c2 = grads(2)
     spread(2, c2)
+    for cp in sent[:early]:
+        cp.wait_send()
     for cp in dq_y:
         cp.wait_recv()
     tot = dys[0].astype(jnp.float32)
@@ -309,6 +312,8 @@
         to = dev(z, y, x, c, up(h, dh, H))
         begin(rcopy(dqf.at[h], dqf.at[h], hss.at[dh - 1], hsr.at[dh - 1], to))
 
+    for cp in sent[early:]:
+        cp.wait_send()
     for hh in range(HL):
         for n, (dz, dh) in enumerate(final):
             rcopy(
@@ -332,8 +337,6 @@
         for p in range(2):
             half = jnp.where(pj // (SLOTS // 2) == p, put, jnp.zeros_like(put))
             parts_ref[p, 0, :, lanes] = mm(half, dqf[i], NN).astype(jnp.bfloat16)
-    for cp in sent:
-        cp.wait_send()
 
 
 def body(X, Y, H, queries, key_states, value_states, attn_output, grad_output, block_index, valid_count):

time: 55.8 us -> 55.6 us (level)
  no operation moved by 1% of the time
where the time goes in v5:
time: 55.6 us; the launch traced here: 55.4 us
  Pallas kernels  52.3 us (94%)
  other arithmetic  1.87 us (3%)
  between operations  1.29 us (2%)
    pallas_call x1, Pallas kernels, body(): pl.pallas_call(functools.partial(kernel, X, Y, H), out_shape=parts, in_sp...  52.3 us
    convert_element_type x1, other arithmetic, body(): (parts[0, a].astype(f32) + parts[1, a].astype(f32)).astype(bf)  1.87 us

profile of v5, /device:TPU:1, one launch (start us, length us, event | category | flops | bytes accessed | tf_op | source)
XLA Modules:
  0.0 55.4 jit_solution(18050042423175445908)
XLA Ops:
  1.3 52.3 %shard_map.94 = bf16[2,3,32,1536]{3,2,1,0:T(8,128)(2,1)} custom-call(s32[1,4]{1,0:T(1,128)} %bi_ref.1, s32[1]{0:T(128)S(6)} %copy.10.vc_ref, bf16[128,384]{1,0:T(8,128)(2,1)} %q_hbm.1, bf16[128,384]{1,0:T(8,128)(2,1)} %k_ref.1, bf16[128,384]{1,0:T(8,128)(2,1)} %v_ref.1, bf16[128,384]{1,0:T(8,128)(2,1)} %o_hbm.1, bf16[128,384]{1,0:T(8,128)(2,1)} %g_hbm.1), custom_call_target="tpu_custom_call" | custom-call | tf_op jit(solution)/shard_map/pallas_call | solution.py:396
  53.6 1.9 %fusion.2 = (bf16[32,1536]{1,0:T(8,128)(2,1)}, bf16[32,1536]{1,0:T(8,128)(2,1)}, bf16[32,1536]{1,0:T(8,128)(2,1)}) fusion(bf16[2,3,32,1536]{3,2,1,0:T(8,128)(2,1)} %shard_map.94), kind=kLoop, calls=%fused_computation.5 | loop fusion | flops 589824 | bytes 884736 | tf_op jit(solution)/shard_map/convert_element_type | solution.py:407

commit v6 on v5

--- a/solution.py
+++ b/solution.py
@@ -37,9 +37,9 @@
     parts_ref,
     q_ref, o_ref, g_ref,
     qbuf, gbuf, kbuf, vbuf, kt, ebuf, dbuf, dqt, mrow, frow, wrow, srow, srow2, sxb, sxl, syb,
-    dqs, rxb, dqo, dys, ryb, dqf, gpart, crecv, fsend, frecv,
+    dqs, rxb, dqo, dys, ryb, dqf, gpart, crecv, fsend, gqv,
     ysend, yrecv, xsend, xrecv, kvsend, kvrecv, ssx, srx, slx, rlx, ssy, sry,
-    dxs, dxr, dss, dsr, css, csr, fss, fsr, hss, hsr, lsem,
+    dxs, dxr, dss, dsr, css, csr, fss, fsr, hss, hsr, lsem, psem,
 ):
     C = Y * SLOTS
     s = lax.axis_index("seq")
@@ -267,6 +267,12 @@
                 gpart[hh, i % 2, a, i // 2] = val[i * TOK : (i + 1) * TOK].astype(jnp.bfloat16)
         return begin(rcopy(gpart.at[hh, 1], crecv.at[hh], css.at[hh], csr.at[hh], core))
 
+    kept = []
+
+    def place(hh, dz, head):
+        lanes = pl.ds(pl.multiple_of(head * FEAT + hh * HD, HD), HD)
+        return parts_ref.at[dz, pl.ds(1, 2), :, lanes]
+
     def spread(hh, cp):
         cp.wait_recv()
         for a in range(2):
@@ -275,10 +281,12 @@
                 fsend[hh, i, :, a] = tot.astype(jnp.bfloat16).reshape(H, TOK // H, HD)
         for n, (dz, dh) in enumerate(final):
             begin(rcopy(
-                fsend.at[hh, dz, up(h, dh, H)], frecv.at[hh, dz, h],
+                fsend.at[hh, dz, up(h, dh, H)], place(hh, dz, h),
                 fss.at[hh, n], fsr.at[hh, n], fp[n],
             ))
-        frecv[hh, 0, h] = fsend[hh, 0, h]
+        cp = pltpu.make_async_copy(fsend.at[hh, 0, h], place(hh, 0, h), psem.at[hh])
+        cp.start()
+        kept.append(cp)
 
     early = len(sent)
     c0 = grads(0)
@@ -312,19 +320,6 @@
         to = dev(z, y, x, c, up(h, dh, H))
         begin(rcopy(dqf.at[h], dqf.at[h], hss.at[dh - 1], hsr.at[dh - 1], to))
 
-    for cp in sent[early:]:
-        cp.wait_send()
-    for hh in range(HL):
-        for n, (dz, dh) in enumerate(final):
-            rcopy(
-                fsend.at[hh, 0, 0], frecv.at[hh, dz, dn(h, dh, H)],
-                fss.at[hh, n], fsr.at[hh, n], fp[n],
-            ).wait_recv()
-        for i in range(H):
-            lanes = slice(i * FEAT + hh * HD, i * FEAT + (hh + 1) * HD)
-            for a in range(2):
-                for p in range(2):
-                    parts_ref[p, a + 1, :, lanes] = frecv[hh, p, i, a]
     for dh in range(1, H):
         slot = dn(h, dh, H)
         rcopy(dqf.at[slot], dqf.at[slot], hss.at[dh - 1], hsr.at[dh - 1], xp[0]).wait_recv()
@@ -336,7 +331,21 @@
         lanes = slice(i * FEAT, (i + 1) * FEAT)
         for p in range(2):
             half = jnp.where(pj // (SLOTS // 2) == p, put, jnp.zeros_like(put))
-            parts_ref[p, 0, :, lanes] = mm(half, dqf[i], NN).astype(jnp.bfloat16)
+            gqv[p, :, lanes] = mm(half, dqf[i], NN).astype(jnp.bfloat16)
+    for p in range(2):
+        cp = pltpu.make_async_copy(gqv.at[p], parts_ref.at[p, 0], psem.at[HL + p])
+        cp.start()
+        kept.append(cp)
+    for cp in sent[early:]:
+        cp.wait_send()
+    for hh in range(HL):
+        for n, (dz, dh) in enumerate(final):
+            rcopy(
+                fsend.at[hh, 0, 0], place(hh, dz, dn(h, dh, H)),
+                fss.at[hh, n], fsr.at[hh, n], fp[n],
+            ).wait_recv()
+    for cp in kept:
+        cp.wait()
 
 
 def body(X, Y, H, queries, key_states, value_states, attn_output, grad_output, block_index, valid_count):
@@ -374,7 +383,7 @@
         V((HL, 2, 2, 2, TOK, HD), bf),
         V((HL, 2, 2, TOK, HD), bf),
         V((HL, 2, H, 2, TOK // H, HD), bf),
-        V((HL, 2, H, 2, TOK // H, HD), bf),
+        V((2, TOK // H, H * FEAT), bf),
         D((2, Y - 1)), D((2, Y - 1)),
         D((2, Y, X - 1)), D((2, Y, X - 1)),
         D((2, 3)), D((2, 3)),
@@ -387,6 +396,7 @@
         D((HL, nf)), D((HL, nf)),
         D((H - 1,)), D((H - 1,)),
         D((5,)),
+        D((HL + 2,)),
     ]
     out = jax.ShapeDtypeStruct((TOK // H, H * FEAT), bf)
     parts = jax.ShapeDtypeStruct((2, 3, TOK // H, H * FEAT), bf)
@@ -397,7 +407,7 @@
         functools.partial(kernel, X, Y, H),
         out_shape=parts,
         in_specs=[sm, sm, hb, hb, hb, hb, hb],
-        out_specs=vm,
+        out_specs=hb,
         scratch_shapes=scratch,
         compiler_params=pltpu.CompilerParams(
             collective_id=0, has_side_effects=True, vmem_limit_bytes=63 * 1024 * 1024

time: 55.6 us -> 55.5 us (level)
  no operation moved by 1% of the time
where the time goes in v6:
time: 55.5 us; the launch traced here: 55.3 us
  Pallas kernels  52.2 us (94%)
  other arithmetic  1.87 us (3%)
  between operations  1.29 us (2%)
    pallas_call x1, Pallas kernels, body(): pl.pallas_call(functools.partial(kernel, X, Y, H), out_shape=parts, in_sp...  52.2 us
    convert_element_type x1, other arithmetic, body(): (parts[0, a].astype(f32) + parts[1, a].astype(f32)).astype(bf)  1.87 us

profile of v6, /device:TPU:1, one launch (start us, length us, event | category | flops | bytes accessed | tf_op | source)
XLA Modules:
  0.0 55.3 jit_solution(7622431581799419267)
XLA Ops:
  1.3 52.2 %shard_map.94 = bf16[2,3,32,1536]{3,2,1,0:T(8,128)(2,1)} custom-call(s32[1,4]{1,0:T(1,128)} %bi_ref.1, s32[1]{0:T(128)S(6)} %copy.10.vc_ref, bf16[128,384]{1,0:T(8,128)(2,1)} %q_hbm.1, bf16[128,384]{1,0:T(8,128)(2,1)} %k_ref.1, bf16[128,384]{1,0:T(8,128)(2,1)} %v_ref.1, bf16[128,384]{1,0:T(8,128)(2,1)} %o_hbm.1, bf16[128,384]{1,0:T(8,128)(2,1)} %g_hbm.1), custom_call_target="tpu_custom_call" | custom-call | tf_op jit(solution)/shard_map/pallas_call | solution.py:406
  53.4 1.9 %fusion.2 = (bf16[32,1536]{1,0:T(8,128)(2,1)}, bf16[32,1536]{1,0:T(8,128)(2,1)}, bf16[32,1536]{1,0:T(8,128)(2,1)}) fusion(bf16[2,3,32,1536]{3,2,1,0:T(8,128)(2,1)} %shard_map.94), kind=kLoop, calls=%fused_computation.5 | loop fusion | flops 589824 | bytes 884736 | tf_op jit(solution)/shard_map/convert_element_type | solution.py:417
